TPU v7x, 32 devices: a whole 2x2x4 slice. The times are simulated.
32 devices in a mesh: parts: 2 (over y), dp: 4 (over z), tensor: 4 (over x, core).
Axes of the slice: x: 2, y: 2, z: 4, core: 2. Of those that a mesh axis runs over, the one named last changes fastest.
Arguments:
- queries: bfloat16 [4096, 8192], P(('parts', 'dp'), 'tensor'), parts along dimension 0, may hold values from -128 to 128
- prefix_key_cache: bfloat16 [2048, 1024], P('parts', 'tensor'), parts along dimension 0, may hold values from -8 to 8
- prefix_value_cache: bfloat16 [2048, 1024], P('parts', 'tensor'), parts along dimension 0, may hold values from -6 to 6
- prompt_keys: bfloat16 [4096, 1024], P(('parts', 'dp'), 'tensor'), parts along dimension 0, may hold values from -6 to 6
- prompt_values: bfloat16 [4096, 1024], P(('parts', 'dp'), 'tensor'), parts along dimension 0, may hold values from -6 to 6
- output_weight: bfloat16 [8192, 4096], P('tensor', 'dp'), may hold values from -1 to 1
- adapter_down_weight: bfloat16 [64, 16, 8192], P(('parts', 'dp'), None, 'tensor'), parts along dimension 0, may hold values from -1 to 1
- adapter_up_weight: bfloat16 [64, 16, 4096], P(('parts', 'dp'), None, 'tensor'), parts along dimension 0, may hold values from -1.5 to 1.5
- adapter_row_map: int32 [64], P('parts'), parts along dimension 0, may hold values from 0 to 31, as said below
- prompt_adapter: int32 [16], P('parts'), parts along dimension 0, may hold values from 0 to 31, as said below
- prompt_length: int32 [16], P('parts'), parts along dimension 0, may hold values from 1 to 256, as said below
- prefix_read_length: int32 [16], P('parts'), parts along dimension 0, may hold values from 2 to 1024, as said below
Outputs:
- projected: bfloat16 [4096, 4096], P(('parts', 'dp'), 'tensor'), parts along dimension 0
There are 2 independent parts, one for each index of `parts`. A program takes and returns all parts, laid end to end along the dimension named above; an argument that names none is the same for every part. Nothing has to cross between parts.
Inputs may be any that keep to these rules, and one draw needn't show every extreme that they name: `adapter_row_map`: a permutation. `prompt_adapter`: among the 2 prompts of one dp group (prompts g * 2 to g * 2 + 1) at most 1 use adapters whose stored rows lie in one and the same group along dp; in every draw some one group stores the adapters of 1 prompts of every dp group. `prompt_length`: some prompt in each draw is full. `prefix_read_length`: some prompt in each draw reads the whole cache.
All inputs are finite; a program needn't handle non-finite values.
Results may differ from a plain program's by a relative error of at most 0.009.
Values may be sent and summed in bfloat16 or wider, within the bound.
A program may use at most 128 MiB of HBM per device.

v0:
```python
import jax
import jax.numpy as jnp
from jax import lax
from jax.sharding import PartitionSpec as P

HD = 128
CAP = 1


adapter_scale = 2.0


def rank_total(partial_value):
    return lax.psum(partial_value, "tensor")


def local_attention(
    queries, prefix_key_cache, prefix_value_cache, prompt_keys, prompt_values, token_prefix
):
    tok_rows, query_width = queries.shape
    positions, key_width = prefix_key_cache.shape
    local_kv = key_width // HD
    group_size = query_width // key_width
    scale = HD ** (-0.5)
    query_four = queries.reshape(tok_rows, local_kv, group_size, HD)
    cache_keys = prefix_key_cache.reshape(positions, local_kv, HD)
    cache_values = prefix_value_cache.reshape(positions, local_kv, HD)
    own_key_heads = prompt_keys.reshape(tok_rows, local_kv, HD)
    own_value_heads = prompt_values.reshape(tok_rows, local_kv, HD)
    scores = (
        jnp.einsum("tkgd,pkd->kgtp", query_four, cache_keys, preferred_element_type=jnp.float32)
        * scale
    )
    own_score = (
        jnp.einsum("tkgd,tkd->kgt", query_four, own_key_heads, preferred_element_type=jnp.float32)
        * scale
    )
    valid = jnp.arange(positions, dtype=jnp.int32)[None, :] < token_prefix[:, None]
    scores = jnp.where(valid[None, None], scores, -jnp.inf)
    highest = jnp.maximum(jnp.max(scores, axis=-1), own_score)
    expon = jnp.exp(scores - highest[..., None])
    own_expon = jnp.exp(own_score - highest)
    total = jnp.sum(expon, axis=-1) + own_expon
    weights = (expon / total[..., None]).astype(jnp.bfloat16)
    own_weight = (own_expon / total).astype(jnp.bfloat16)
    context = jnp.einsum(
        "kgtp,pkd->tkgd", weights, cache_values, preferred_element_type=jnp.float32
    )
    context = context + jnp.einsum(
        "kgt,tkd->tkgd", own_weight, own_value_heads, preferred_element_type=jnp.float32
    )
    return context.reshape(tok_rows, query_width).astype(jnp.bfloat16)


def selected_blocks(local_adapter_index, adapter_down_weight, adapter_up_weight):
    adapter_number = adapter_down_weight.shape[0]
    adapter_selector = (
        local_adapter_index[..., None] == jnp.arange(adapter_number, dtype=jnp.int32)
    ).astype(jnp.bfloat16)
    down_selected = jnp.einsum(
        "ljm,mes->ljes", adapter_selector, adapter_down_weight, preferred_element_type=jnp.float32
    ).astype(jnp.bfloat16)
    up_selected = jnp.einsum(
        "yuv,vzj->yuzj", adapter_selector, adapter_up_weight, preferred_element_type=jnp.float32
    ).astype(jnp.bfloat16)
    return (down_selected, up_selected)


def local(
    queries,
    prefix_key_cache,
    prefix_value_cache,
    prompt_keys,
    prompt_values,
    output_weight,
    adapter_down_weight,
    adapter_up_weight,
    adapter_row_map,
    prompt_adapter,
    prompt_length,
    prefix_read_length,
):
    group_count = lax.axis_size("dp")
    group = lax.axis_index("dp")
    tok_rows, query_width = queries.shape
    prompt_count = prompt_length.shape[0] // group_count
    seg_rows = tok_rows // prompt_count
    first_prompt = group * prompt_count
    my_lengths = lax.dynamic_slice_in_dim(prompt_length, first_prompt, prompt_count)
    my_prefix = lax.dynamic_slice_in_dim(prefix_read_length, first_prompt, prompt_count)
    token_prefix = jnp.repeat(my_prefix, seg_rows, total_repeat_length=tok_rows)
    context = local_attention(
        queries, prefix_key_cache, prefix_value_cache, prompt_keys, prompt_values, token_prefix
    )
    token_length = jnp.repeat(my_lengths, seg_rows, total_repeat_length=tok_rows)
    live_rows = jnp.arange(tok_rows, dtype=jnp.int32) % seg_rows < token_length
    context = context * live_rows.astype(jnp.bfloat16)[:, None]
    partial_value = jnp.dot(
        context,
        lax.all_gather(output_weight, "dp", axis=1, tiled=True),
        preferred_element_type=jnp.float32,
    )
    base_output = lax.psum_scatter(partial_value, "tensor", scatter_dimension=1, tiled=True)
    adapter_count = adapter_row_map.shape[0]
    adapter_local_row = adapter_down_weight.shape[0]
    matches = prompt_adapter[:, None] == jnp.arange(adapter_count, dtype=jnp.int32)[None, :]
    stored_all = jnp.sum(jnp.where(matches, adapter_row_map[None, :], 0), axis=1)
    owners = (stored_all // adapter_local_row).reshape(group_count, prompt_count)
    local_rows = (stored_all % adapter_local_row).reshape(group_count, prompt_count)
    same_owner = owners[:, :, None] == owners[:, None, :]
    earlier = jnp.arange(prompt_count)[None, None, :] < jnp.arange(prompt_count)[None, :, None]
    slots = jnp.sum(same_owner & earlier, axis=2)
    my_owner = lax.dynamic_index_in_dim(owners, group, 0, keepdims=False)
    my_slot = lax.dynamic_index_in_dim(slots, group, 0, keepdims=False)
    context_seg = context.reshape(prompt_count, seg_rows, query_width)
    owner_ids = jnp.arange(group_count, dtype=jnp.int32)
    slot_ids = jnp.arange(CAP, dtype=jnp.int32)
    give_mask = (owners == group)[:, None, :] & (slots[:, None, :] == slot_ids[None, :, None])
    which_give = jnp.sum(jnp.where(give_mask, local_rows[:, None, :], 0), axis=2)
    down_send, up_send = selected_blocks(which_give, adapter_down_weight, adapter_up_weight)
    down_recv, up_recv = (
        lax.all_to_all(down_send, "dp", split_axis=0, concat_axis=0, tiled=True),
        lax.all_to_all(up_send, "dp", split_axis=0, concat_axis=0, tiled=True),
    )
    take = (
        (my_owner[:, None, None] == owner_ids[None, :, None])
        & (my_slot[:, None, None] == slot_ids[None, None, :])
    ).astype(jnp.bfloat16)
    down_mine = jnp.einsum(
        "sdc,dcrf->srf", take, down_recv, preferred_element_type=jnp.float32
    ).astype(jnp.bfloat16)
    up_mine = jnp.einsum("sdc,dcro->sro", take, up_recv, preferred_element_type=jnp.float32).astype(
        jnp.bfloat16
    )
    lowrank = rank_total(
        jnp.einsum("sxf,srf->sxr", context_seg, down_mine, preferred_element_type=jnp.float32)
    ).astype(jnp.bfloat16)
    adapter_delta = jnp.einsum(
        "sxr,sro->sxo", lowrank, up_mine, preferred_element_type=jnp.float32
    ).astype(jnp.bfloat16)
    adapter_delta = adapter_delta.reshape(tok_rows, adapter_delta.shape[-1])
    projected = base_output + adapter_scale * adapter_delta.astype(jnp.float32)
    return projected.astype(jnp.bfloat16)


def solution(mesh):
    in_specs = (
        P(("parts", "dp"), "tensor"),
        P("parts", "tensor"),
        P("parts", "tensor"),
        P(("parts", "dp"), "tensor"),
        P(("parts", "dp"), "tensor"),
        P("tensor", "dp"),
        P(("parts", "dp"), None, "tensor"),
        P(("parts", "dp"), None, "tensor"),
        P("parts"),
        P("parts"),
        P("parts"),
        P("parts"),
    )
    out_specs = P(("parts", "dp"), "tensor")
    return jax.shard_map(local, mesh=mesh, in_specs=in_specs, out_specs=out_specs, check_vma=False)
```

profile of v0, /device:TPU:0, one launch (start us, length us, event | category | flops | bytes accessed | tf_op | source)
XLA Modules:
  0.0 394.0 jit_solution(1525146539434457560)
XLA Ops:
  6.5 0.7 all-gather.2.cloned.1.call-update
  7.3 2.2 copy.89
  9.5 1.2 reshape.368
  10.8 1.7 reshape.399
  12.5 3.0 fusion.10
  15.5 1.1 copy.82
  16.6 0.9 copy.88
  17.6 2.1 copy.87
  19.7 0.1 dynamic_slice.13
  19.8 0.1 dynamic_slice.14
  19.8 0.7 fusion.51
  20.5 0.6 fusion.50
  21.1 1.3 fusion.35
  22.4 1.3 broadcast_select_fusion
  23.7 0.4 iota_compare_fusion
  24.0 14.3 %fusion.1 = (f32[2,8,512]{2,1,0:T(8,128)S(1)}, f32[2,1024,512,8]{2,1,3,0:T(8,128)}) fusion(pred[512,1024]{0,1:T(8,128)(4,1)S(1)} %iota_compare_fusion, bf16[512,2,8,128]{3,2,1,0:T(8,128)(2,1)S(1)} %bitcast.100, bf16[1024,2,128,1]{2,1,0,3:T(2,128)(2,1)S(1)} %bitcast.101), kind=kOutput, calls=%fused_computation.4 | convolution fusion | flops 2172641280 | bytes 36732928 | tf_op jit(solution)/shard_map/tkgd,pkd->kgtp/dot_general | solution.py:31
  38.4 14.6 %fusion = f32[2,8,512]{2,1,0:T(8,128)S(1)} fusion(f32[2,1024,512,8]{2,1,3,0:T(8,128)} %get-tuple-element.33, f32[2,8,512]{2,1,0:T(8,128)S(1)} %bitcast_maximum_fusion, pred[512,1024]{0,1:T(8,128)(4,1)S(1)} %iota_compare_fusion), kind=kLoop, calls=%fused_computation.3 | loop fusion | flops 33546240 | bytes 34144256 | tf_op jit(solution)/shard_map/reduce_sum | solution.py:43
  53.0 15.5 %fusion.3 = bf16[512,2,8,128]{0,3,2,1:T(8,128)(2,1)S(1)} fusion(bf16[1024,2,128,1]{0,2,3,1:T(8,128)(2,1)S(1)} %bitcast.104, f32[2,1024,512,8]{2,1,3,0:T(8,128)} %get-tuple-element.33, f32[2,8,512]{2,1,0:T(8,128)S(1)} %get-tuple-element.27, f32[2,8,512]{2,1,0:T(8,128)S(1)} %bitcast_maximum_fusion, pred[512,1024]{0,1:T(8,128)(4,1)S(1)} %iota_compare_fusion, ...), kind=kOutput, calls=%fused_computation.7 | convolution fusion | flops 2192572416 | bytes 37322752 | tf_op jit(solution)/shard_map/kgtp,pkd->tkgd/dot_general | solution.py:46
  68.6 1.7 bitcast_multiply_fusion
  70.2 228.2 %all-gather.2.cloned.1.call-done = bf16[2048,4096]{1,0:T(8,128)(2,1)} async-done(((bf16[2048,1024]{1,0:T(8,128)(2,1)}), bf16[2048,4096]{1,0:T(8,128)(2,1)}) %all-gather.2.cloned.1.call-update) | async-done | bytes 16777232 | tf_op jit(solution)/shard_map/all_gather | solution.py:100
  298.4 15.2 %fusion.52 = f32[512,4096]{1,0:T(8,128)} fusion(bf16[512,2048]{0,1:T(8,128)(2,1)} %bitcast_multiply_fusion, bf16[2048,4096]{1,0:T(8,128)(2,1)} %all-gather.2.cloned.1.call-done), kind=kOutput, calls=%fused_computation.91 | convolution fusion | flops 8589934592 | bytes 27262976 | tf_op jit(solution)/shard_map/dot_general | solution.py:98
  313.6 0.6 copy-done.8
  314.3 0.2 select_reduce_fusion
  314.5 0.1 reduce_sum.42
  314.5 0.1 reduce_sum.44
  314.6 0.1 copy.66
  314.7 0.1 fusion.31
  314.8 0.1 copy.70
  315.0 0.1 fusion.30
  315.1 0.3 fusion.12
  315.4 0.7 copy.76
  316.1 3.3 all-to-all-start.1
  319.4 0.5 fusion.4
  319.9 0.9 copy.72
  320.7 5.0 %all-to-all-done.1 = bf16[4,1,16,1024]{3,2,1,0:T(8,128)(2,1)S(1)} async-done(((bf16[4,1,16,1024]{3,2,1,0:T(8,128)(2,1)}), bf16[4,1,16,1024]{3,2,1,0:T(8,128)(2,1)S(1)}, u32[]{:S(2)}, u32[]{:S(2)}) %all-to-all-start.1) | async-done | bytes 131104 | tf_op jit(solution)/shard_map/all_to_all | solution.py:123
  325.8 3.4 all-to-all-start
  329.2 2.1 convert_element_type.60
  331.3 4.8 %copy.65 = bf16[2,256,2048]{2,1,0:T(8,128)(2,1)S(1)} copy(bf16[2,256,2048]{1,0,2:T(2,128)(2,1)} %convert_element_type.60) | data formatting | bytes 4194304 | tf_op jit(solution)/shard_map/convert_element_type | solution.py:52
  336.1 0.2 dynamic-slice_reduce_fusion
  336.3 0.2 compare_reduce_fusion
  336.5 0.3 convolution_convert_fusion.4
  336.8 0.6 all-to-all-done
  337.3 0.4 convolution_convert_fusion.1
  337.7 0.7 fusion.8
  338.4 11.6 %psum.7 = bf16[2,256,16]{1,2,0:T(8,128)(2,1)S(1)} all-reduce(f32[2,256,16]{1,2,0:T(8,128)S(1)} %fusion.8), channel_id=1, replica_groups=mesh['parts'=2,'dp'=4,'tensor'=4] {'tensor'}, use_global_device_ids=true, to_apply=%region_6.8 | all-reduce | flops 8192 | bytes 49152 | tf_op jit(solution)/shard_map/psum | solution.py:14
  350.0 0.5 convert_multiply_fusion
  350.5 33.8 %reduce-scatter.2.cloned.1.call-done = f32[512,1024]{1,0:T(8,128)} async-done(((f32[512,4096]{1,0:T(8,128)}), f32[512,1024]{1,0:T(8,128)}) %reduce-scatter.2.cloned.1.call-update) | async-done | bytes 2097168 | tf_op jit(solution)/shard_map/reduce_scatter | solution.py:103
  384.3 2.9 fusion.5
  (28 shorter events, 0.2 us)
Async XLA Ops:
  6.5 312.9 %copy-start = (bf16[8,16,2048]{2,1,0:T(8,128)(2,1)S(1)}, bf16[8,16,2048]{2,1,0:T(8,128)(2,1)}, u32[]{:S(2)}) copy-start(bf16[8,16,2048]{2,1,0:T(8,128)(2,1)} %param.24) | copy-start | bytes 1572868
  6.5 291.9 %all-gather.2.cloned.1.call-start = ((), (), s32[]{:S(2)}) async-start(), calls=%async_computation.3 | async-start | bytes 20971520 | tf_op jit(solution)/shard_map/all_gather | solution.py:100
  7.3 377.0 %reduce-scatter.2.cloned.1.call-start = ((), (), s32[]{:S(2)}) async-start(), calls=%async_computation.4 | async-start | bytes 10485760 | tf_op jit(solution)/shard_map/reduce_scatter | solution.py:103
  9.5 7.1 %copy-start.3 = (bf16[512,256]{1,0:T(8,128)(2,1)S(1)}, bf16[512,256]{1,0:T(8,128)(2,1)}, u32[]{:S(2)}) copy-start(bf16[512,256]{1,0:T(8,128)(2,1)} %param.22) | copy-start | bytes 786436
  10.7 8.9 %copy-start.6 = (s32[8]{0:T(128)S(1)}, s32[8]{0:T(128)}, u32[]{:S(2)}) copy-start(s32[8]{0:T(128)} %param.29) | copy-start | bytes 100
  10.8 9.0 %copy-start.7 = (s32[8]{0:T(128)S(1)}, s32[8]{0:T(128)}, u32[]{:S(2)}) copy-start(s32[8]{0:T(128)} %param.28) | copy-start | bytes 100
  10.8 10.4 %copy-start.5 = (pred[512]{0:T(512)(128)(4,1)S(1)}, pred[512]{0:T(512)(128)(4,1)}, u32[]{:S(2)}) copy-start(pred[512]{0:T(512)(128)(4,1)} %constant.172) | copy-start | bytes 1540
  38.4 14.6 %copy-start.1 = (f32[512,256]{0,1:T(8,128)S(1)}, f32[512,256]{0,1:T(8,128)}, u32[]{:S(2)}) copy-start(f32[512,256]{0,1:T(8,128)} %copy.88) | copy-start | bytes 1572868
  38.4 14.6 %copy-start.2 = (bf16[1024,256]{0,1:T(8,128)(2,1)S(1)}, bf16[1024,256]{0,1:T(8,128)(2,1)}, u32[]{:S(2)}) copy-start(bf16[1024,256]{0,1:T(8,128)(2,1)} %copy.87) | copy-start | bytes 1572868
  313.6 0.7 copy-start.8
  313.6 0.7 copy-start.9
  313.6 1.5 copy-start.4
  316.1 9.7 %all-to-all-start.1 = ((bf16[4,1,16,1024]{3,2,1,0:T(8,128)(2,1)}), bf16[4,1,16,1024]{3,2,1,0:T(8,128)(2,1)S(1)}, u32[]{:S(2)}, u32[]{:S(2)}) async-start(bf16[4,1,16,1024]{3,2,1,0:T(8,128)(2,1)} %copy.76), calls=%async_computation.2 | async-start | bytes 262144 | tf_op jit(solution)/shard_map/all_to_all | solution.py:123
  325.8 11.6 %all-to-all-start = ((bf16[4,1,16,2048]{3,2,1,0:T(8,128)(2,1)}), bf16[4,1,16,2048]{3,2,1,0:T(8,128)(2,1)S(1)}, u32[]{:S(2)}, u32[]{:S(2)}) async-start(bf16[4,1,16,2048]{3,2,1,0:T(8,128)(2,1)} %copy.72), calls=%async_computation.1 | async-start | bytes 524288 | tf_op jit(solution)/shard_map/all_to_all | solution.py:122
Sparse Core Ops, SparseCore 0:
  8.9 289.4 all-gather.1
  313.8 70.4 reduce-scatter.1
where the time goes:
time: 395 us; the launch traced here: 394 us
  waiting for transfers between devices  268 us (68%)
  matrix products  50.6 us (13%)
  other arithmetic  22.7 us (6%)
  local copies, waits for them, and re-layouts  20.4 us (5%)
  between operations  13.6 us (3%)
  blocking collectives  11.6 us (3%)
  starting transfers between devices  6.78 us (2%)
    all_gather x1, waiting for transfers between devices, local(): lax.all_gather(output_weight, 'dp', axis=1, tiled=True)  228 us
    reduce_scatter x1, waiting for transfers between devices, local(): lax.psum_scatter(partial_value, 'tensor', scatter_dimension=1, tiled=True)  33.8 us
    dot_general x1, matrix products, local_attention(): jnp.einsum('kgtp,pkd->tkgd', weights, cache_values, preferred_element_typ...  15.5 us
    dot_general x1, matrix products, local(): jnp.dot(context, lax.all_gather(output_weight, 'dp', axis=1, tiled=True),...  15.2 us
    reduce_sum x1, other arithmetic, local_attention(): total = jnp.sum(expon, axis=-1) + own_expon  14.6 us
    dot_general x1, matrix products, local_attention(): jnp.einsum('tkgd,pkd->kgtp', query_four, cache_keys, preferred_element_ty...  14.3 us
    psum x1, blocking collectives, rank_total(): return lax.psum(partial_value, 'tensor')  11.6 us
  transfers between devices with their start and end apart: 4, of which 4 were waited for; matrix products, arithmetic and copies ran while one was open for 19% of the time, Pallas kernels for 0%

commit v1 on v0

--- a/solution.py
+++ b/solution.py
@@ -5,6 +5,7 @@
 
 HD = 128
 CAP = 1
+PIECES = 2
 
 
 adapter_scale = 2.0
@@ -83,6 +84,18 @@
     group_count = lax.axis_size("dp")
     group = lax.axis_index("dp")
     tok_rows, query_width = queries.shape
+    part_count = lax.axis_size("parts")
+    half_rows = query_width // part_count
+    piece_width = output_weight.shape[1] // PIECES
+    half_weight = lax.dynamic_slice_in_dim(
+        output_weight, lax.axis_index("parts") * half_rows, half_rows, axis=0
+    )
+    gathered_weights = [
+        lax.all_gather(
+            half_weight[:, piece * piece_width : (piece + 1) * piece_width], ("dp", "parts"), axis=0
+        )
+        for piece in range(PIECES)
+    ]
     prompt_count = prompt_length.shape[0] // group_count
     seg_rows = tok_rows // prompt_count
     first_prompt = group * prompt_count
@@ -95,12 +108,6 @@
     token_length = jnp.repeat(my_lengths, seg_rows, total_repeat_length=tok_rows)
     live_rows = jnp.arange(tok_rows, dtype=jnp.int32) % seg_rows < token_length
     context = context * live_rows.astype(jnp.bfloat16)[:, None]
-    partial_value = jnp.dot(
-        context,
-        lax.all_gather(output_weight, "dp", axis=1, tiled=True),
-        preferred_element_type=jnp.float32,
-    )
-    base_output = lax.psum_scatter(partial_value, "tensor", scatter_dimension=1, tiled=True)
     adapter_count = adapter_row_map.shape[0]
     adapter_local_row = adapter_down_weight.shape[0]
     matches = prompt_adapter[:, None] == jnp.arange(adapter_count, dtype=jnp.int32)[None, :]
@@ -139,6 +146,23 @@
         "sxr,sro->sxo", lowrank, up_mine, preferred_element_type=jnp.float32
     ).astype(jnp.bfloat16)
     adapter_delta = adapter_delta.reshape(tok_rows, adapter_delta.shape[-1])
+    context, adapter_delta = lax.optimization_barrier((context, adapter_delta))
+    context_parts = context.reshape(tok_rows, part_count * half_rows)
+    pieces = []
+    for gathered in gathered_weights:
+        blocks = gathered.reshape(group_count, query_width, piece_width)
+        partial_value = jnp.concatenate(
+            [
+                jnp.dot(context_parts, blocks[index], preferred_element_type=jnp.float32)
+                for index in range(group_count)
+            ],
+            axis=1,
+        )
+        summed = lax.psum_scatter(
+            partial_value.astype(jnp.bfloat16), "tensor", scatter_dimension=1, tiled=True
+        )
+        pieces.append(summed.reshape(tok_rows, -1, 1, piece_width))
+    base_output = jnp.concatenate(pieces, axis=2).reshape(tok_rows, -1).astype(jnp.float32)
     projected = base_output + adapter_scale * adapter_delta.astype(jnp.float32)
     return projected.astype(jnp.bfloat16)
 

time: 395 us -> 348 us (0.88)
  waiting for transfers between devices: 268 us -> 201 us
  matrix products: 50.6 us -> 56.6 us
  other arithmetic: 22.7 us -> 28 us
  local copies, waits for them, and re-layouts: 20.4 us -> 25.4 us
  starting transfers between devices: 6.78 us -> 11.7 us
    all_gather x1 -> x2, waiting for transfers between devices: 228 us -> 138 us  [local(): lax.all_gather(half_weight[:, piece * piece_width:(piece + 1) * piece_wid...]
    reduce_scatter x1 -> x2, waiting for transfers between devices: 33.8 us -> 56 us  [local(): lax.psum_scatter(partial_value.astype(jnp.bfloat16), 'tensor', scatter_di...]
    all_to_all x1, waiting for transfers between devices: 0.59 us -> 6.15 us  [local(): lax.all_to_all(down_send, 'dp', split_axis=0, concat_axis=0, tiled=True)]
    all_to_all x1, waiting for transfers between devices: 5.04 us -> 0.01 us  [local(): lax.all_to_all(up_send, 'dp', split_axis=0, concat_axis=0, tiled=True)]
    concatenate x0 -> x3, other arithmetic: none -> 4.21 us  [the longest x2 2.92 us: local(): jnp.concatenate([jnp.dot(context_parts, blocks[index], preferred_element_...]
    dot_general x1 -> x8, matrix products: 15.2 us -> 17.3 us  [local(): jnp.dot(context_parts, blocks[index], preferred_element_type=jnp.float32)]
  transfers between devices with their start and end apart: 4 -> 6, of which waited for: 4 -> 5; matrix products, arithmetic and copies ran while one was open for 19% -> 29% of each run, Pallas kernels for 0% -> 0%
where the time goes in v1:
time: 348 us; the launch traced here: 347 us
  waiting for transfers between devices  201 us (58%)
  matrix products  56.6 us (16%)
  other arithmetic  28 us (8%)
  local copies, waits for them, and re-layouts  25.4 us (7%)
  between operations  13.4 us (4%)
  starting transfers between devices  11.7 us (3%)
  blocking collectives  11.1 us (3%)
    all_gather x2, waiting for transfers between devices, local(): lax.all_gather(half_weight[:, piece * piece_width:(piece + 1) * piece_wid...  138 us
    reduce_scatter x2, waiting for transfers between devices, local(): lax.psum_scatter(partial_value.astype(jnp.bfloat16), 'tensor', scatter_di...  56 us
    dot_general x8, matrix products, local(): jnp.dot(context_parts, blocks[index], preferred_element_type=jnp.float32)  17.3 us
    dot_general x1, matrix products, local_attention(): jnp.einsum('kgtp,pkd->tkgd', weights, cache_values, preferred_element_typ...  16.4 us
    reduce_sum x1, other arithmetic, local_attention(): total = jnp.sum(expon, axis=-1) + own_expon  14.5 us
    dot_general x1, matrix products, local_attention(): jnp.einsum('tkgd,pkd->kgtp', query_four, cache_keys, preferred_element_ty...  13.7 us
    psum x1, blocking collectives, rank_total(): return lax.psum(partial_value, 'tensor')  11.1 us
    convert_element_type x2, local copies, waits for them, and re-layouts, local_attention(): return context.reshape(tok_rows, query_width).astype(jnp.bfloat16)  8.2 us
  transfers between devices with their start and end apart: 6, of which 5 were waited for; matrix products, arithmetic and copies ran while one was open for 29% of the time, Pallas kernels for 0%

profile of v1, /device:TPU:0, one launch (start us, length us, event | category | flops | bytes accessed | tf_op | source)
XLA Modules:
  0.0 347.1 jit_solution(13125999025700687622)
XLA Ops:
  6.5 3.1 constant_dynamic-slice_fusion
  9.7 0.7 all-gather.7.cloned.1.call-update
  11.5 0.7 copy.80
  12.2 6.3 %all-to-all-start.1 = ((bf16[4,1,16,1024]{3,2,1,0:T(8,128)(2,1)}), bf16[4,1,16,1024]{3,2,1,0:T(8,128)(2,1)}, u32[]{:S(2)}, u32[]{:S(2)}) async-start(bf16[4,1,16,1024]{3,2,1,0:T(8,128)(2,1)} %copy.80), calls=%async_computation.1 | async-start | bytes 262144 | tf_op jit(solution)/shard_map/all_to_all | solution.py:130
  18.6 2.5 copy.94
  21.0 1.2 reshape.394
  22.3 0.8 reshape.447
  23.0 3.0 fusion.25
  26.0 1.2 copy.87
  27.2 0.9 copy.93
  28.2 2.1 copy.92
  30.2 0.5 fusion.4
  30.7 0.9 copy.76
  31.7 0.6 fusion.90
  32.3 0.6 fusion.89
  33.0 1.2 broadcast_select_fusion
  34.2 0.4 iota_compare_fusion
  34.5 13.7 %fusion.1 = (f32[2,8,512]{2,1,0:T(8,128)S(1)}, f32[2,1024,512,8]{2,1,3,0:T(8,128)}) fusion(pred[512,1024]{0,1:T(8,128)(4,1)S(1)} %iota_compare_fusion, bf16[512,2,8,128]{3,2,1,0:T(8,128)(2,1)S(1)} %bitcast.108, bf16[1024,2,128,1]{2,1,0,3:T(2,128)(2,1)S(1)} %bitcast.110), kind=kOutput, calls=%fused_computation.4 | convolution fusion | flops 2172641280 | bytes 36732928 | tf_op jit(solution)/shard_map/tkgd,pkd->kgtp/dot_general | solution.py:32
  48.3 14.5 %fusion = f32[2,8,512]{2,1,0:T(8,128)S(1)} fusion(f32[2,1024,512,8]{2,1,3,0:T(8,128)} %get-tuple-element.39, f32[2,8,512]{2,1,0:T(8,128)S(1)} %bitcast_maximum_fusion, pred[512,1024]{0,1:T(8,128)(4,1)S(1)} %iota_compare_fusion), kind=kLoop, calls=%fused_computation.3 | loop fusion | flops 33546240 | bytes 34144256 | tf_op jit(solution)/shard_map/reduce_sum | solution.py:44
  62.8 16.4 %fusion.3 = bf16[512,2,8,128]{0,3,2,1:T(8,128)(2,1)S(1)} fusion(bf16[1024,2,128,1]{0,2,3,1:T(8,128)(2,1)S(1)} %bitcast.113, f32[2,1024,512,8]{2,1,3,0:T(8,128)} %get-tuple-element.39, f32[2,8,512]{2,1,0:T(8,128)S(1)} %get-tuple-element.33, f32[2,8,512]{2,1,0:T(8,128)S(1)} %bitcast_maximum_fusion, pred[512,1024]{0,1:T(8,128)(4,1)S(1)} %iota_compare_fusion, ...), kind=kOutput, calls=%fused_computation.7 | convolution fusion | flops 2192572416 | bytes 37322752 | tf_op jit(solution)/shard_map/kgtp,pkd->tkgd/dot_general | solution.py:47
  79.2 1.2 fusion.74
  80.5 5.1 %all-to-all-start = ((bf16[4,1,16,2048]{3,2,1,0:T(8,128)(2,1)}), bf16[4,1,16,2048]{3,2,1,0:T(8,128)(2,1)S(1)}, u32[]{:S(2)}, u32[]{:S(2)}) async-start(bf16[4,1,16,2048]{3,2,1,0:T(8,128)(2,1)} %copy.76), calls=%async_computation | async-start | bytes 524288 | tf_op jit(solution)/shard_map/all_to_all | solution.py:129
  85.5 1.6 bitcast_multiply_fusion
  87.2 2.0 convert_element_type.67
  89.2 6.2 %copy.69 = bf16[2,256,2048]{2,1,0:T(8,128)(2,1)} copy(bf16[2,256,2048]{1,0,2:T(2,128)(2,1)} %convert_element_type.67) | data formatting | bytes 4194304 | tf_op jit(solution)/shard_map/convert_element_type | solution.py:53
  95.7 1.2 convolution_convert_fusion.4
  96.9 6.1 %all-to-all-done = bf16[4,1,16,2048]{3,2,1,0:T(8,128)(2,1)S(1)} async-done(((bf16[4,1,16,2048]{3,2,1,0:T(8,128)(2,1)}), bf16[4,1,16,2048]{3,2,1,0:T(8,128)(2,1)S(1)}, u32[]{:S(2)}, u32[]{:S(2)}) %all-to-all-start) | async-done | bytes 262176 | tf_op jit(solution)/shard_map/all_to_all | solution.py:129
  103.4 2.4 fusion.23
  105.9 11.1 %psum.7 = bf16[2,256,16]{1,2,0:T(8,128)(2,1)S(1)} all-reduce(f32[2,256,16]{1,2,0:T(8,128)S(1)} %fusion.23), channel_id=1, replica_groups=mesh['parts'=2,'dp'=4,'tensor'=4] {'tensor'}, use_global_device_ids=true, to_apply=%region_5.7 | all-reduce | flops 8192 | bytes 49152 | tf_op jit(solution)/shard_map/psum | solution.py:15
  117.0 1.4 convolution_convert_fusion.2
  118.4 22.2 %all-gather.5.cloned.1.call-done = bf16[8192,512]{1,0:T(8,128)(2,1)} async-done(((bf16[1024,512]{1,0:T(8,128)(2,1)}), bf16[8192,512]{1,0:T(8,128)(2,1)}) %all-gather.5.cloned.1.call-update) | async-done | bytes 8388624 | tf_op jit(solution)/shard_map/all_gather | solution.py:94
  140.6 3.0 fusion.27
  143.7 3.0 fusion.30
  146.8 1.3 fusion.33
  148.1 1.3 fusion.36
  149.4 1.5 pad_maximum_fusion
  151.1 115.7 %all-gather.7.cloned.1.call-done = bf16[8192,512]{1,0:T(8,128)(2,1)} async-done(((bf16[1024,512]{1,0:T(8,128)(2,1)}), bf16[8192,512]{1,0:T(8,128)(2,1)}) %all-gather.7.cloned.1.call-update) | async-done | bytes 8388624 | tf_op jit(solution)/shard_map/all_gather | solution.py:94
  266.8 3.0 fusion.39
  269.9 3.0 fusion.42
  272.9 1.3 fusion.45
  274.2 1.3 fusion.48
  275.5 1.4 pad_maximum_fusion.1
  277.0 22.0 %reduce-scatter.3.cloned.1.call-done = bf16[512,512]{0,1:T(8,128)(2,1)} async-done(((bf16[512,2048]{0,1:T(8,128)(2,1)}), bf16[512,512]{0,1:T(8,128)(2,1)}) %reduce-scatter.3.cloned.1.call-update) | async-done | bytes 524304 | tf_op jit(solution)/shard_map/reduce_scatter | solution.py:161
  299.0 34.0 %reduce-scatter.5.cloned.1.call-done = bf16[512,512]{0,1:T(8,128)(2,1)} async-done(((bf16[512,2048]{0,1:T(8,128)(2,1)}), bf16[512,512]{0,1:T(8,128)(2,1)}) %reduce-scatter.5.cloned.1.call-update) | async-done | bytes 524304 | tf_op jit(solution)/shard_map/reduce_scatter | solution.py:161
  333.0 1.3 pad_maximum_fusion.2
  334.3 1.7 bitcast_convert_fusion
  336.0 2.0 copy.83
  338.0 2.6 add_convert_fusion
  (63 shorter events, 2.4 us)
Async XLA Ops:
  6.5 23.7 %copy-start = (bf16[8,16,2048]{2,1,0:T(8,128)(2,1)S(1)}, bf16[8,16,2048]{2,1,0:T(8,128)(2,1)}, u32[]{:S(2)}) copy-start(bf16[8,16,2048]{2,1,0:T(8,128)(2,1)} %param.24) | copy-start | bytes 1572868
  6.5 134.1 %all-gather.5.cloned.1.call-start = ((), (), s32[]{:S(2)}) async-start(), calls=%async_computation.6 | async-start | bytes 9437184 | tf_op jit(solution)/shard_map/all_gather | solution.py:94
  9.6 0.8 copy-start.9
  9.6 0.8 copy-start.10
  9.6 1.6 copy-start.6
  9.6 257.2 %all-gather.7.cloned.1.call-start = ((), (), s32[]{:S(2)}) async-start(), calls=%async_computation.7 | async-start | bytes 9437184 | tf_op jit(solution)/shard_map/all_gather | solution.py:94
  12.2 68.2 %all-to-all-start.1 = ((bf16[4,1,16,1024]{3,2,1,0:T(8,128)(2,1)}), bf16[4,1,16,1024]{3,2,1,0:T(8,128)(2,1)}, u32[]{:S(2)}, u32[]{:S(2)}) async-start(bf16[4,1,16,1024]{3,2,1,0:T(8,128)(2,1)} %copy.80), calls=%async_computation.1 | async-start | bytes 262144 | tf_op jit(solution)/shard_map/all_to_all | solution.py:130
  18.6 3.7 %copy-start.7 = (bf16[512,256]{1,0:T(8,128)(2,1)S(1)}, bf16[512,256]{1,0:T(8,128)(2,1)}, u32[]{:S(2)}) copy-start(bf16[512,256]{1,0:T(8,128)(2,1)} %param.21) | copy-start | bytes 786436
  23.0 4.2 %copy-start.5 = (bf16[512,256]{1,0:T(8,128)(2,1)S(1)}, bf16[512,256]{1,0:T(8,128)(2,1)}, u32[]{:S(2)}) copy-start(bf16[512,256]{1,0:T(8,128)(2,1)} %param.22) | copy-start | bytes 786436
  26.0 5.5 %copy-start.11 = (s32[8]{0:T(128)S(1)}, s32[8]{0:T(128)}, u32[]{:S(2)}) copy-start(s32[8]{0:T(128)} %param.29) | copy-start | bytes 100
  26.0 5.6 %copy-start.12 = (s32[8]{0:T(128)S(1)}, s32[8]{0:T(128)}, u32[]{:S(2)}) copy-start(s32[8]{0:T(128)} %param.28) | copy-start | bytes 100
  26.0 6.9 %copy-start.8 = (pred[512]{0:T(512)(128)(4,1)S(1)}, pred[512]{0:T(512)(128)(4,1)}, u32[]{:S(2)}) copy-start(pred[512]{0:T(512)(128)(4,1)} %constant.182) | copy-start | bytes 1540
  48.3 14.5 %copy-start.3 = (f32[512,256]{0,1:T(8,128)S(1)}, f32[512,256]{0,1:T(8,128)}, u32[]{:S(2)}) copy-start(f32[512,256]{0,1:T(8,128)} %copy.93) | copy-start | bytes 1572868
  48.3 14.5 %copy-start.4 = (bf16[1024,256]{0,1:T(8,128)(2,1)S(1)}, bf16[1024,256]{0,1:T(8,128)(2,1)}, u32[]{:S(2)}) copy-start(bf16[1024,256]{0,1:T(8,128)(2,1)} %copy.92) | copy-start | bytes 1572868
  80.5 22.6 %all-to-all-start = ((bf16[4,1,16,2048]{3,2,1,0:T(8,128)(2,1)}), bf16[4,1,16,2048]{3,2,1,0:T(8,128)(2,1)S(1)}, u32[]{:S(2)}, u32[]{:S(2)}) async-start(bf16[4,1,16,2048]{3,2,1,0:T(8,128)(2,1)} %copy.76), calls=%async_computation | async-start | bytes 524288 | tf_op jit(solution)/shard_map/all_to_all | solution.py:129
  85.5 213.4 %reduce-scatter.3.cloned.1.call-start = ((), (), s32[]{:S(2)}) async-start(), calls=%async_computation.4 | async-start | bytes 2621440 | tf_op jit(solution)/shard_map/reduce_scatter | solution.py:161
  103.4 37.2 %copy-start.2 = (bf16[512,2048]{0,1:T(8,128)(2,1)S(1)}, bf16[512,2048]{0,1:T(8,128)(2,1)}, u32[]{:S(2)}) copy-start(bf16[512,2048]{0,1:T(8,128)(2,1)} %bitcast_multiply_fusion) | copy-start | bytes 6291460
  140.6 6.1 %slice-start.2 = ((s8[8388608]{0:T(1024)(128)(4,1)}), s8[4194304]{0:T(1024)(128)(4,1)S(1)}, s32[]{:S(2)}) async-start(s8[8388608]{0:T(1024)(128)(4,1)} %bitcast.118), calls=%async_computation.10 | async-start | bytes 8388608
  143.7 3.1 slice-start.3
  150.8 182.1 %reduce-scatter.5.cloned.1.call-start = ((), (), s32[]{:S(2)}) async-start(), calls=%async_computation.5 | async-start | bytes 2621440 | tf_op jit(solution)/shard_map/reduce_scatter | solution.py:161
  266.8 6.1 %slice-start = ((s8[8388608]{0:T(1024)(128)(4,1)}), s8[4194304]{0:T(1024)(128)(4,1)S(1)}, s32[]{:S(2)}) async-start(s8[8388608]{0:T(1024)(128)(4,1)} %bitcast.116), calls=%async_computation.8 | async-start | bytes 8388608
  269.8 3.1 slice-start.1
  336.0 4.5 %copy-start.1 = (bf16[8,16,2048]{2,1,0:T(8,128)(2,1)S(1)}, bf16[8,16,2048]{2,1,0:T(8,128)(2,1)}, u32[]{:S(2)}) copy-start(bf16[8,16,2048]{2,1,0:T(8,128)(2,1)} %param.24) | copy-start | bytes 1572868
Sparse Core Ops, SparseCore 0:
  9.8 130.8 all-gather.4
  142.8 124.0 all-gather.6
  269.3 29.5 reduce-scatter.2
  301.5 31.4 reduce-scatter.4

commit v2 on v0

--- a/solution.py
+++ b/solution.py
@@ -5,6 +5,7 @@
 
 HD = 128
 CAP = 1
+PIECES = 2
 
 
 adapter_scale = 2.0
@@ -64,6 +65,67 @@
         "yuv,vzj->yuzj", adapter_selector, adapter_up_weight, preferred_element_type=jnp.float32
     ).astype(jnp.bfloat16)
     return (down_selected, up_selected)
+
+
+def chain_gather(pieces_in):
+    group = lax.axis_index("dp")
+    up = [(0, 1), (1, 2), (2, 3)]
+    down = [(1, 0), (2, 1), (3, 2)]
+    swap = [(0, 1), (1, 0)]
+    count = len(pieces_in)
+    from_low = list(pieces_in)
+    from_high = list(pieces_in)
+    first_high = [None] * count
+    slots = [[] for _ in range(count)]
+    for step in range(1, 4):
+        for piece in range(count):
+            from_low[piece] = lax.ppermute(from_low[piece], "dp", up)
+            from_high[piece] = lax.ppermute(from_high[piece], "dp", down)
+            low, high = from_low[piece], from_high[piece]
+            if step == 1:
+                first_high[piece] = high
+                mine = jnp.where(group >= 1, low, high)
+            elif step == 2:
+                mine = jnp.where(group >= 2, low, high)
+            else:
+                mine = jnp.where(
+                    group == 3, low, jnp.where(group == 0, high, first_high[piece])
+                )
+            slots[piece].append((mine, lax.ppermute(mine, "parts", swap)))
+    return slots
+
+
+def chain_project(context, own, slots):
+    group = lax.axis_index("dp")
+    part = lax.axis_index("parts")
+    tensor = lax.axis_index("tensor")
+    core, chip = tensor % 2, tensor // 2
+    half = own.shape[0] // 2
+    context_mine = lax.dynamic_slice_in_dim(context, part * half, half, axis=1)
+    context_other = lax.dynamic_slice_in_dim(context, (1 - part) * half, half, axis=1)
+    results = [jnp.dot(context, own, preferred_element_type=jnp.float32).astype(jnp.bfloat16)]
+    for mine, other in slots:
+        value = jnp.dot(context_mine, mine, preferred_element_type=jnp.float32)
+        value = value + jnp.dot(context_other, other, preferred_element_type=jnp.float32)
+        results.append(value.astype(jnp.bfloat16))
+    stack = jnp.stack(results)
+    first = jnp.where(group >= 1, group - 1, 1)
+    second = jnp.where(group >= 2, group - 2, group + 2)
+    third = jnp.where(group == 3, 0, jnp.where(group == 0, 3, group + 1))
+    order = jnp.stack([group, first, second, third])
+
+    def block(index):
+        slot = jnp.sum(jnp.where(order == index, jnp.arange(4, dtype=jnp.int32), 0))
+        return lax.dynamic_index_in_dim(stack, slot, 0, keepdims=False)
+
+    core_swap = [(0, 1), (1, 0), (2, 3), (3, 2)]
+    chip_swap = [(0, 2), (2, 0), (1, 3), (3, 1)]
+    far = jnp.stack([block(1 - core), block(3 - core)])
+    far = lax.ppermute(far, "tensor", core_swap).astype(jnp.float32)
+    near = jnp.stack([block(core), block(2 + core)]).astype(jnp.float32) + far
+    sent = lax.dynamic_index_in_dim(near, 1 - chip, 0, keepdims=False).astype(jnp.bfloat16)
+    kept = lax.dynamic_index_in_dim(near, chip, 0, keepdims=False)
+    return kept + lax.ppermute(sent, "tensor", chip_swap).astype(jnp.float32)
 
 
 def local(
@@ -83,6 +145,20 @@
     group_count = lax.axis_size("dp")
     group = lax.axis_index("dp")
     tok_rows, query_width = queries.shape
+    part_count = lax.axis_size("parts")
+    half_rows = query_width // part_count
+    piece_width = output_weight.shape[1] // PIECES
+    half_weight = lax.dynamic_slice_in_dim(
+        output_weight, lax.axis_index("parts") * half_rows, half_rows, axis=0
+    )
+    pieces_in = [
+        half_weight[:, piece * piece_width : (piece + 1) * piece_width] for piece in range(PIECES)
+    ]
+    chained = group_count == 4 and part_count == 2 and lax.axis_size("tensor") == 4
+    if chained:
+        gathered_weights = chain_gather(pieces_in)
+    else:
+        gathered_weights = [lax.all_gather(piece, ("dp", "parts"), axis=0) for piece in pieces_in]
     prompt_count = prompt_length.shape[0] // group_count
     seg_rows = tok_rows // prompt_count
     first_prompt = group * prompt_count
@@ -95,12 +171,6 @@
     token_length = jnp.repeat(my_lengths, seg_rows, total_repeat_length=tok_rows)
     live_rows = jnp.arange(tok_rows, dtype=jnp.int32) % seg_rows < token_length
     context = context * live_rows.astype(jnp.bfloat16)[:, None]
-    partial_value = jnp.dot(
-        context,
-        lax.all_gather(output_weight, "dp", axis=1, tiled=True),
-        preferred_element_type=jnp.float32,
-    )
-    base_output = lax.psum_scatter(partial_value, "tensor", scatter_dimension=1, tiled=True)
     adapter_count = adapter_row_map.shape[0]
     adapter_local_row = adapter_down_weight.shape[0]
     matches = prompt_adapter[:, None] == jnp.arange(adapter_count, dtype=jnp.int32)[None, :]
@@ -139,6 +209,20 @@
         "sxr,sro->sxo", lowrank, up_mine, preferred_element_type=jnp.float32
     ).astype(jnp.bfloat16)
     adapter_delta = adapter_delta.reshape(tok_rows, adapter_delta.shape[-1])
+    context, adapter_delta = lax.optimization_barrier((context, adapter_delta))
+    pieces = []
+    for piece, gathered in enumerate(gathered_weights):
+        if chained:
+            own = output_weight[:, piece * piece_width : (piece + 1) * piece_width]
+            summed = chain_project(context, own, gathered)
+        else:
+            blocks = gathered.reshape(group_count, query_width, piece_width)
+            partial_value = jnp.einsum(
+                "tf,dfc->tdc", context, blocks, preferred_element_type=jnp.float32
+            ).reshape(tok_rows, -1)
+            summed = lax.psum_scatter(partial_value, "tensor", scatter_dimension=1, tiled=True)
+        pieces.append(summed.reshape(tok_rows, -1, 1, piece_width))
+    base_output = jnp.concatenate(pieces, axis=2).reshape(tok_rows, -1)
     projected = base_output + adapter_scale * adapter_delta.astype(jnp.float32)
     return projected.astype(jnp.bfloat16)
 

time: 395 us -> 337 us (0.85)
  waiting for transfers between devices: 268 us -> 136 us
  starting transfers between devices: 6.78 us -> 61.2 us
  other arithmetic: 22.7 us -> 37.2 us
  local copies, waits for them, and re-layouts: 20.4 us -> 29.5 us
  between operations: 13.6 us -> 8.01 us
    all_gather x1 -> x0, waiting for transfers between devices: 228 us -> none  [local(): lax.all_gather(output_weight, 'dp', axis=1, tiled=True)]
    ppermute x0 -> x22, waiting for transfers between devices: none -> 136 us  [the longest x6 88.7 us: chain_gather(): slots[piece].append((mine, lax.ppermute(mine, 'parts', swap)))]
    ppermute x0 -> x22, starting transfers between devices: none -> 49.4 us  [the longest x6 30.8 us: chain_gather(): from_low[piece] = lax.ppermute(from_low[piece], 'dp', up)]
    reduce_scatter x1 -> x0, waiting for transfers between devices: 33.8 us -> none  [local(): lax.psum_scatter(partial_value, 'tensor', scatter_dimension=1, tiled=True)]
    select_n x0 -> x4, other arithmetic: none -> 5.81 us  [the longest x2 3.13 us: chain_gather(): mine = jnp.where(group >= 1, low, high)]
    all_to_all x1, waiting for transfers between devices: 5.04 us -> 0.01 us  [local(): lax.all_to_all(up_send, 'dp', split_axis=0, concat_axis=0, tiled=True)]
    dot_general x1 -> x14, matrix products: 15.2 us -> 13.4 us  [the longest x6 4.63 us: chain_project(): value = jnp.dot(context_mine, mine, preferred_element_type=jnp.float32)]
  transfers between devices with their start and end apart: 4 -> 24, of which waited for: 4 -> 12; matrix products, arithmetic and copies ran while one was open for 19% -> 31% of each run, Pallas kernels for 0% -> 0%
where the time goes in v2:
time: 337 us; the launch traced here: 335 us
  waiting for transfers between devices  136 us (40%)
  starting transfers between devices  61.2 us (18%)
  matrix products  51.8 us (15%)
  other arithmetic  37.2 us (11%)
  local copies, waits for them, and re-layouts  29.5 us (9%)
  blocking collectives  11.1 us (3%)
  between operations  8.01 us (2%)
    ppermute x6, waiting for transfers between devices, chain_gather(): slots[piece].append((mine, lax.ppermute(mine, 'parts', swap)))  88.7 us
    ppermute x6, starting transfers between devices, chain_gather(): from_low[piece] = lax.ppermute(from_low[piece], 'dp', up)  30.8 us
    ppermute x6, waiting for transfers between devices, chain_gather(): from_low[piece] = lax.ppermute(from_low[piece], 'dp', up)  21.9 us
    ppermute x2, waiting for transfers between devices, chain_project(): return kept + lax.ppermute(sent, 'tensor', chip_swap).astype(jnp.float32)  19.2 us
    dot_general x1, matrix products, local_attention(): jnp.einsum('kgtp,pkd->tkgd', weights, cache_values, preferred_element_typ...  15.6 us
    dot_general x1, matrix products, local_attention(): jnp.einsum('tkgd,pkd->kgtp', query_four, cache_keys, preferred_element_ty...  14.6 us
    reduce_sum x1, other arithmetic, local_attention(): total = jnp.sum(expon, axis=-1) + own_expon  14.4 us
    psum x1, blocking collectives, rank_total(): return lax.psum(partial_value, 'tensor')  11.1 us
  transfers between devices with their start and end apart: 24, of which 12 were waited for; matrix products, arithmetic and copies ran while one was open for 31% of the time, Pallas kernels for 0%

profile of v2, /device:TPU:0, one launch (start us, length us, event | category | flops | bytes accessed | tf_op | source)
XLA Modules:
  0.0 335.1 jit_solution(5368993885695488646)
XLA Ops:
  0.0 3.1 constant_dynamic-slice_fusion
  3.1 5.9 %collective-permute-start = (bf16[1024,512]{1,0:T(8,128)(2,1)}, bf16[1024,512]{1,0:T(8,128)(2,1)}, u32[]{:S(2)}, u32[]{:S(2)}) collective-permute-start(bf16[1024,512]{1,0:T(8,128)(2,1)} %get-tuple-element.34), channel_id=1, source_target_pairs={{0,4},{4,8},{8,12},{1,5},{5,9},{9,13},{2,6},{6,10},{10,14},{3,7},{... | collective-permute-start | bytes 3145736 | tf_op jit(solution)/shard_map/ppermute | solution.py:82
  10.3 5.5 %collective-permute-start.11 = (bf16[1024,512]{1,0:T(8,128)(2,1)}, bf16[1024,512]{1,0:T(8,128)(2,1)}, u32[]{:S(2)}, u32[]{:S(2)}) collective-permute-start(bf16[1024,512]{1,0:T(8,128)(2,1)} %get-tuple-element.35), channel_id=1, source_target_pairs={{0,4},{4,8},{8,12},{1,5},{5,9},{9,13},{2,6},{6,10},{10,14},{3,7},{... | collective-permute-start | bytes 3145736 | tf_op jit(solution)/shard_map/ppermute | solution.py:82
  19.0 6.0 %all-to-all-start.1 = ((bf16[4,1,16,1024]{3,2,1,0:T(8,128)(2,1)}), bf16[4,1,16,1024]{3,2,1,0:T(8,128)(2,1)S(1)}, u32[]{:S(2)}, u32[]{:S(2)}) async-start(bf16[4,1,16,1024]{3,2,1,0:T(8,128)(2,1)} %copy.80), calls=%async_computation.1 | async-start | bytes 262144 | tf_op jit(solution)/shard_map/all_to_all | solution.py:193
  27.4 2.2 copy.94
  29.7 2.0 reshape.378
  32.4 3.0 fusion.13
  36.5 14.6 %fusion.1 = (f32[2,8,512]{2,1,0:T(8,128)S(1)}, f32[2,1024,512,8]{2,1,3,0:T(8,128)}) fusion(pred[512,1024]{0,1:T(8,128)(4,1)S(1)} %iota_compare_fusion, bf16[512,2,8,128]{3,2,1,0:T(8,128)(2,1)S(1)} %bitcast.146, bf16[1024,2,128,1]{2,1,0,3:T(2,128)(2,1)} %bitcast.149), kind=kOutput, calls=%fused_computation.4 | convolution fusion | flops 2172641280 | bytes 36732928 | tf_op jit(solution)/shard_map/tkgd,pkd->kgtp/dot_general | solution.py:32
  51.1 14.4 %fusion = f32[2,8,512]{2,1,0:T(8,128)S(1)} fusion(f32[2,1024,512,8]{2,1,3,0:T(8,128)} %get-tuple-element.55, f32[2,8,512]{2,1,0:T(8,128)S(1)} %bitcast_maximum_fusion, pred[512,1024]{0,1:T(8,128)(4,1)S(1)} %iota_compare_fusion), kind=kLoop, calls=%fused_computation.3 | loop fusion | flops 33546240 | bytes 34144256 | tf_op jit(solution)/shard_map/reduce_sum | solution.py:44
  67.5 15.6 %fusion.3 = bf16[512,2,8,128]{0,3,2,1:T(8,128)(2,1)S(1)} fusion(bf16[1024,2,128,1]{0,2,3,1:T(8,128)(2,1)} %bitcast.152, f32[2,1024,512,8]{2,1,3,0:T(8,128)} %get-tuple-element.55, f32[2,8,512]{2,1,0:T(8,128)S(1)} %get-tuple-element.49, f32[2,8,512]{2,1,0:T(8,128)S(1)} %bitcast_maximum_fusion, pred[512,1024]{0,1:T(8,128)(4,1)S(1)} %iota_compare_fusion, ...), kind=kOutput, calls=%fused_computation.7 | convolution fusion | flops 2192572416 | bytes 37322752 | tf_op jit(solution)/shard_map/kgtp,pkd->tkgd/dot_general | solution.py:47
  86.5 4.9 %collective-permute-start.3 = (bf16[1024,512]{1,0:T(8,128)(2,1)}, bf16[1024,512]{1,0:T(8,128)(2,1)}, u32[]{:S(2)}, u32[]{:S(2)}) collective-permute-start(bf16[1024,512]{1,0:T(8,128)(2,1)} %collective-permute-done), channel_id=1, source_target_pairs={{0,4},{4,8},{8,12},{1,5},{5,9},{9,13},{2,6},{6,10},{10,14},{3,7},{... | collective-permute-start | bytes 3145736 | tf_op jit(solution)/shard_map/ppermute | solution.py:82
  92.8 5.7 %all-to-all-start = ((bf16[4,1,16,2048]{3,2,1,0:T(8,128)(2,1)}), bf16[4,1,16,2048]{3,2,1,0:T(8,128)(2,1)S(1)}, u32[]{:S(2)}, u32[]{:S(2)}) async-start(bf16[4,1,16,2048]{3,2,1,0:T(8,128)(2,1)} %copy.76), calls=%async_computation | async-start | bytes 524288 | tf_op jit(solution)/shard_map/all_to_all | solution.py:192
  98.5 1.6 bitcast_multiply_fusion
  100.1 2.0 convert_element_type.113
  108.0 6.2 %copy.69 = bf16[2,256,2048]{2,1,0:T(8,128)(2,1)} copy(bf16[2,256,2048]{1,0,2:T(2,128)(2,1)} %convert_element_type.113) | data formatting | bytes 4194304 | tf_op jit(solution)/shard_map/convert_element_type | solution.py:53
  117.3 4.9 %collective-permute-start.14 = (bf16[1024,512]{1,0:T(8,128)(2,1)}, bf16[1024,512]{1,0:T(8,128)(2,1)}, u32[]{:S(2)}, u32[]{:S(2)}) collective-permute-start(bf16[1024,512]{1,0:T(8,128)(2,1)} %collective-permute-done.11), channel_id=1, source_target_pairs={{0,4},{4,8},{8,12},{1,5},{5,9},{9,13},{2,6},{6,10},{10,14},{3,7},{... | collective-permute-start | bytes 3145736 | tf_op jit(solution)/shard_map/ppermute | solution.py:82
  123.9 2.4 fusion.11
  126.4 11.1 %psum.7 = bf16[2,256,16]{1,2,0:T(8,128)(2,1)S(1)} all-reduce(f32[2,256,16]{1,2,0:T(8,128)S(1)} %fusion.11), channel_id=1, replica_groups=mesh['parts'=2,'dp'=4,'tensor'=4] {'tensor'}, use_global_device_ids=true, to_apply=%region_5.7 | all-reduce | flops 8192 | bytes 49152 | tf_op jit(solution)/shard_map/psum | solution.py:15
  137.5 1.4 convolution_convert_fusion.2
  138.9 4.9 %collective-permute-start.6 = (bf16[1024,512]{1,0:T(8,128)(2,1)}, bf16[1024,512]{1,0:T(8,128)(2,1)S(1)}, u32[]{:S(2)}, u32[]{:S(2)}) collective-permute-start(bf16[1024,512]{1,0:T(8,128)(2,1)} %collective-permute-done.3), channel_id=1, source_target_pairs={{0,4},{4,8},{8,12},{1,5},{5,9},{9,13},{2,6},{6,10},{10,14},{3,7},{... | collective-permute-start | bytes 3145736 | tf_op jit(solution)/shard_map/ppermute | solution.py:82
  145.1 2.9 fusion.30
  148.0 4.6 %collective-permute-start.17 = (bf16[1024,512]{1,0:T(8,128)(2,1)}, bf16[1024,512]{1,0:T(8,128)(2,1)S(1)}, u32[]{:S(2)}, u32[]{:S(2)}) collective-permute-start(bf16[1024,512]{1,0:T(8,128)(2,1)} %collective-permute-done.14), channel_id=1, source_target_pairs={{0,4},{4,8},{8,12},{1,5},{5,9},{9,13},{2,6},{6,10},{10,14},{3,7},{... | collective-permute-start | bytes 3145736 | tf_op jit(solution)/shard_map/ppermute | solution.py:82
  155.2 1.4 broadcast_select_fusion.1
  156.6 1.6 collective-permute-start.5
  158.2 1.3 broadcast_select_fusion
  159.5 8.1 %collective-permute-done.6 = bf16[1024,512]{1,0:T(8,128)(2,1)S(1)} collective-permute-done((bf16[1024,512]{1,0:T(8,128)(2,1)}, bf16[1024,512]{1,0:T(8,128)(2,1)S(1)}, u32[]{:S(2)}, u32[]{:S(2)}) %collective-permute-start.6) | collective-permute-done | bytes 1048608 | tf_op jit(solution)/shard_map/ppermute | solution.py:82
  167.6 1.5 collective-permute-start.16
  169.1 2.9 collective-permute-done.7
  172.0 1.6 broadcast_select_fusion.3
  173.5 1.6 collective-permute-start.2
  175.1 13.8 %collective-permute-done.17 = bf16[1024,512]{1,0:T(8,128)(2,1)S(1)} collective-permute-done((bf16[1024,512]{1,0:T(8,128)(2,1)}, bf16[1024,512]{1,0:T(8,128)(2,1)S(1)}, u32[]{:S(2)}, u32[]{:S(2)}) %collective-permute-start.17) | collective-permute-done | bytes 1048608 | tf_op jit(solution)/shard_map/ppermute | solution.py:82
  189.0 1.5 collective-permute-start.8
  190.5 2.6 collective-permute-done.18
  193.1 1.6 broadcast_select_fusion.2
  194.6 1.6 collective-permute-start.13
  198.3 7.0 %collective-permute-done.16 = bf16[1024,512]{1,0:T(8,128)(2,1)S(1)} collective-permute-done((bf16[1024,512]{1,0:T(8,128)(2,1)S(1)}, bf16[1024,512]{1,0:T(8,128)(2,1)S(1)}, u32[]{:S(2)}, u32[]{:S(2)}) %collective-permute-start.16) | collective-permute-done | bytes 1048608 | tf_op jit(solution)/shard_map/ppermute | solution.py:94
  206.8 20.9 %collective-permute-done.2 = bf16[1024,512]{1,0:T(8,128)(2,1)S(1)} collective-permute-done((bf16[1024,512]{1,0:T(8,128)(2,1)S(1)}, bf16[1024,512]{1,0:T(8,128)(2,1)S(1)}, u32[]{:S(2)}, u32[]{:S(2)}) %collective-permute-start.2) | collective-permute-done | bytes 1048608 | tf_op jit(solution)/shard_map/ppermute | solution.py:94
  228.5 21.7 %collective-permute-done.8 = bf16[1024,512]{1,0:T(8,128)(2,1)S(1)} collective-permute-done((bf16[1024,512]{1,0:T(8,128)(2,1)S(1)}, bf16[1024,512]{1,0:T(8,128)(2,1)S(1)}, u32[]{:S(2)}, u32[]{:S(2)}) %collective-permute-start.8) | collective-permute-done | bytes 1048608 | tf_op jit(solution)/shard_map/ppermute | solution.py:94
  252.5 20.1 %collective-permute-done.13 = bf16[1024,512]{1,0:T(8,128)(2,1)S(1)} collective-permute-done((bf16[1024,512]{1,0:T(8,128)(2,1)S(1)}, bf16[1024,512]{1,0:T(8,128)(2,1)S(1)}, u32[]{:S(2)}, u32[]{:S(2)}) %collective-permute-start.13) | collective-permute-done | bytes 1048608 | tf_op jit(solution)/shard_map/ppermute | solution.py:94
  274.2 18.9 %collective-permute-done.19 = bf16[1024,512]{1,0:T(8,128)(2,1)S(1)} collective-permute-done((bf16[1024,512]{1,0:T(8,128)(2,1)S(1)}, bf16[1024,512]{1,0:T(8,128)(2,1)S(1)}, u32[]{:S(2)}, u32[]{:S(2)}) %collective-permute-start.19) | collective-permute-done | bytes 1048608 | tf_op jit(solution)/shard_map/ppermute | solution.py:94
  295.2 1.4 constant_dynamic-slice_fusion.4
  300.4 1.9 convert_add_fusion.1
  304.1 1.6 convert_add_fusion
  305.7 1.3 copy-done.1
  308.3 10.0 %collective-permute-done.10 = bf16[512,512]{0,1:T(8,128)(2,1)} collective-permute-done((bf16[512,512]{0,1:T(8,128)(2,1)}, bf16[512,512]{0,1:T(8,128)(2,1)}, u32[]{:S(2)}, u32[]{:S(2)}) %collective-permute-start.10) | collective-permute-done | bytes 524320 | tf_op jit(solution)/shard_map/ppermute | solution.py:128
  319.5 9.2 %collective-permute-done.21 = bf16[512,512]{0,1:T(8,128)(2,1)} collective-permute-done((bf16[512,512]{0,1:T(8,128)(2,1)S(1)}, bf16[512,512]{0,1:T(8,128)(2,1)}, u32[]{:S(2)}, u32[]{:S(2)}) %collective-permute-start.21) | collective-permute-done | bytes 524320 | tf_op jit(solution)/shard_map/ppermute | solution.py:128
  330.1 1.8 copy.83
  331.9 3.2 add_convert_fusion
  (110 shorter events, 42.0 us)
Async XLA Ops:
  0.0 83.2 %copy-start = (bf16[8,16,2048]{2,1,0:T(8,128)(2,1)S(1)}, bf16[8,16,2048]{2,1,0:T(8,128)(2,1)}, u32[]{:S(2)}) copy-start(bf16[8,16,2048]{2,1,0:T(8,128)(2,1)} %param.24) | copy-start | bytes 1572868
  0.0 17.2 %copy-start.12 = (s32[32]{0:T(128)S(1)}, s32[32]{0:T(128)}, u32[]{:S(2)}) copy-start(s32[32]{0:T(128)} %param.26) | copy-start | bytes 388
  0.0 17.2 %copy-start.13 = (s32[8]{0:T(128)S(1)}, s32[8]{0:T(128)}, u32[]{:S(2)}) copy-start(s32[8]{0:T(128)} %param.27) | copy-start | bytes 100
  0.0 18.0 %copy-start.9 = (bf16[8,16,1024]{2,1,0:T(8,128)(2,1)S(1)}, bf16[8,16,1024]{2,1,0:T(8,128)(2,1)}, u32[]{:S(2)}) copy-start(bf16[8,16,1024]{2,1,0:T(8,128)(2,1)} %param.25) | copy-start | bytes 786436
  0.0 25.0 %copy-start.14 = (s32[8]{0:T(128)S(1)}, s32[8]{0:T(128)}, u32[]{:S(2)}) copy-start(s32[8]{0:T(128)} %param.29) | copy-start | bytes 100
  0.0 25.7 %copy-start.11 = (pred[512]{0:T(512)(128)(4,1)S(1)}, pred[512]{0:T(512)(128)(4,1)}, u32[]{:S(2)}) copy-start(pred[512]{0:T(512)(128)(4,1)} %constant.241) | copy-start | bytes 1540
  3.1 83.4 %collective-permute-start = (bf16[1024,512]{1,0:T(8,128)(2,1)}, bf16[1024,512]{1,0:T(8,128)(2,1)}, u32[]{:S(2)}, u32[]{:S(2)}) collective-permute-start(bf16[1024,512]{1,0:T(8,128)(2,1)} %get-tuple-element.34), channel_id=1, source_target_pairs={{0,4},{4,8},{8,12},{1,5},{5,9},{9,13},{2,6},{6,10},{10,14},{3,7},{... | collective-permute-start | bytes 3145736 | tf_op jit(solution)/shard_map/ppermute | solution.py:82
  9.0 82.4 %collective-permute-start.1 = (bf16[1024,512]{1,0:T(8,128)(2,1)}, bf16[1024,512]{1,0:T(8,128)(2,1)}, u32[]{:S(2)}, u32[]{:S(2)}) collective-permute-start(bf16[1024,512]{1,0:T(8,128)(2,1)} %get-tuple-element.34), channel_id=1, source_target_pairs={{4,0},{8,4},{12,8},{5,1},{9,5},{13,9},{6,2},{10,6},{14,10},{7,3},{... | collective-permute-start | bytes 3145736 | tf_op jit(solution)/shard_map/ppermute | solution.py:83
  10.3 107.0 %collective-permute-start.11 = (bf16[1024,512]{1,0:T(8,128)(2,1)}, bf16[1024,512]{1,0:T(8,128)(2,1)}, u32[]{:S(2)}, u32[]{:S(2)}) collective-permute-start(bf16[1024,512]{1,0:T(8,128)(2,1)} %get-tuple-element.35), channel_id=1, source_target_pairs={{0,4},{4,8},{8,12},{1,5},{5,9},{9,13},{2,6},{6,10},{10,14},{3,7},{... | collective-permute-start | bytes 3145736 | tf_op jit(solution)/shard_map/ppermute | solution.py:82
  15.9 106.4 %collective-permute-start.12 = (bf16[1024,512]{1,0:T(8,128)(2,1)}, bf16[1024,512]{1,0:T(8,128)(2,1)}, u32[]{:S(2)}, u32[]{:S(2)}) collective-permute-start(bf16[1024,512]{1,0:T(8,128)(2,1)} %get-tuple-element.35), channel_id=1, source_target_pairs={{4,0},{8,4},{12,8},{5,1},{9,5},{13,9},{6,2},{10,6},{14,10},{7,3},{... | collective-permute-start | bytes 3145736 | tf_op jit(solution)/shard_map/ppermute | solution.py:83
  19.0 73.8 %all-to-all-start.1 = ((bf16[4,1,16,1024]{3,2,1,0:T(8,128)(2,1)}), bf16[4,1,16,1024]{3,2,1,0:T(8,128)(2,1)S(1)}, u32[]{:S(2)}, u32[]{:S(2)}) async-start(bf16[4,1,16,1024]{3,2,1,0:T(8,128)(2,1)} %copy.80), calls=%async_computation.1 | async-start | bytes 262144 | tf_op jit(solution)/shard_map/all_to_all | solution.py:193
  27.4 4.2 %copy-start.10 = (bf16[512,256]{1,0:T(8,128)(2,1)S(1)}, bf16[512,256]{1,0:T(8,128)(2,1)}, u32[]{:S(2)}) copy-start(bf16[512,256]{1,0:T(8,128)(2,1)} %param.21) | copy-start | bytes 786436
  51.1 14.5 %copy-start.8 = (bf16[512,256]{1,0:T(8,128)(2,1)S(1)}, bf16[512,256]{1,0:T(8,128)(2,1)}, u32[]{:S(2)}) copy-start(bf16[512,256]{1,0:T(8,128)(2,1)} %param.22) | copy-start | bytes 786436
  51.1 15.4 %copy-start.7 = (bf16[1024,256]{1,0:T(8,128)(2,1)S(1)}, bf16[1024,256]{1,0:T(8,128)(2,1)}, u32[]{:S(2)}) copy-start(bf16[1024,256]{1,0:T(8,128)(2,1)} %param.20) | copy-start | bytes 1572868
  67.5 15.6 %copy-start.15 = (s32[8]{0:T(128)S(1)}, s32[8]{0:T(128)}, u32[]{:S(2)}) copy-start(s32[8]{0:T(128)} %param.28) | copy-start | bytes 100
  86.5 52.4 %collective-permute-start.3 = (bf16[1024,512]{1,0:T(8,128)(2,1)}, bf16[1024,512]{1,0:T(8,128)(2,1)}, u32[]{:S(2)}, u32[]{:S(2)}) collective-permute-start(bf16[1024,512]{1,0:T(8,128)(2,1)} %collective-permute-done), channel_id=1, source_target_pairs={{0,4},{4,8},{8,12},{1,5},{5,9},{9,13},{2,6},{6,10},{10,14},{3,7},{... | collective-permute-start | bytes 3145736 | tf_op jit(solution)/shard_map/ppermute | solution.py:82
  91.5 52.3 %collective-permute-start.4 = (bf16[1024,512]{1,0:T(8,128)(2,1)}, bf16[1024,512]{1,0:T(8,128)(2,1)}, u32[]{:S(2)}, u32[]{:S(2)}) collective-permute-start(bf16[1024,512]{1,0:T(8,128)(2,1)} %collective-permute-done.1), channel_id=1, source_target_pairs={{4,0},{8,4},{12,8},{5,1},{9,5},{13,9},{6,2},{10,6},{14,10},{7,3},{... | collective-permute-start | bytes 3145736 | tf_op jit(solution)/shard_map/ppermute | solution.py:83
  92.8 30.8 %all-to-all-start = ((bf16[4,1,16,2048]{3,2,1,0:T(8,128)(2,1)}), bf16[4,1,16,2048]{3,2,1,0:T(8,128)(2,1)S(1)}, u32[]{:S(2)}, u32[]{:S(2)}) async-start(bf16[4,1,16,2048]{3,2,1,0:T(8,128)(2,1)} %copy.76), calls=%async_computation | async-start | bytes 524288 | tf_op jit(solution)/shard_map/all_to_all | solution.py:192
  117.3 30.7 %collective-permute-start.14 = (bf16[1024,512]{1,0:T(8,128)(2,1)}, bf16[1024,512]{1,0:T(8,128)(2,1)}, u32[]{:S(2)}, u32[]{:S(2)}) collective-permute-start(bf16[1024,512]{1,0:T(8,128)(2,1)} %collective-permute-done.11), channel_id=1, source_target_pairs={{0,4},{4,8},{8,12},{1,5},{5,9},{9,13},{2,6},{6,10},{10,14},{3,7},{... | collective-permute-start | bytes 3145736 | tf_op jit(solution)/shard_map/ppermute | solution.py:82
  122.3 30.4 %collective-permute-start.15 = (bf16[1024,512]{1,0:T(8,128)(2,1)}, bf16[1024,512]{1,0:T(8,128)(2,1)}, u32[]{:S(2)}, u32[]{:S(2)}) collective-permute-start(bf16[1024,512]{1,0:T(8,128)(2,1)} %collective-permute-done.12), channel_id=1, source_target_pairs={{4,0},{8,4},{12,8},{5,1},{9,5},{13,9},{6,2},{10,6},{14,10},{7,3},{... | collective-permute-start | bytes 3145736 | tf_op jit(solution)/shard_map/ppermute | solution.py:83
  123.9 21.2 %copy-start.3 = (bf16[512,2048]{0,1:T(8,128)(2,1)S(1)}, bf16[512,2048]{0,1:T(8,128)(2,1)}, u32[]{:S(2)}) copy-start(bf16[512,2048]{0,1:T(8,128)(2,1)} %bitcast_multiply_fusion) | copy-start | bytes 6291460
  138.9 15.0 %copy-start.5 = (bf16[2048,1024]{1,0:T(8,128)(2,1)S(1)}, bf16[2048,1024]{1,0:T(8,128)(2,1)}, u32[]{:S(2)}) copy-start(bf16[2048,1024]{1,0:T(8,128)(2,1)} %param.23) | copy-start | bytes 12582916
  138.9 28.7 %collective-permute-start.6 = (bf16[1024,512]{1,0:T(8,128)(2,1)}, bf16[1024,512]{1,0:T(8,128)(2,1)S(1)}, u32[]{:S(2)}, u32[]{:S(2)}) collective-permute-start(bf16[1024,512]{1,0:T(8,128)(2,1)} %collective-permute-done.3), channel_id=1, source_target_pairs={{0,4},{4,8},{8,12},{1,5},{5,9},{9,13},{2,6},{6,10},{10,14},{3,7},{... | collective-permute-start | bytes 3145736 | tf_op jit(solution)/shard_map/ppermute | solution.py:82
  143.8 28.2 %collective-permute-start.7 = (bf16[1024,512]{1,0:T(8,128)(2,1)}, bf16[1024,512]{1,0:T(8,128)(2,1)S(1)}, u32[]{:S(2)}, u32[]{:S(2)}) collective-permute-start(bf16[1024,512]{1,0:T(8,128)(2,1)} %collective-permute-done.4), channel_id=1, source_target_pairs={{4,0},{8,4},{12,8},{5,1},{9,5},{13,9},{6,2},{10,6},{14,10},{7,3},{... | collective-permute-start | bytes 3145736 | tf_op jit(solution)/shard_map/ppermute | solution.py:83
  148.0 41.0 %collective-permute-start.17 = (bf16[1024,512]{1,0:T(8,128)(2,1)}, bf16[1024,512]{1,0:T(8,128)(2,1)S(1)}, u32[]{:S(2)}, u32[]{:S(2)}) collective-permute-start(bf16[1024,512]{1,0:T(8,128)(2,1)} %collective-permute-done.14), channel_id=1, source_target_pairs={{0,4},{4,8},{8,12},{1,5},{5,9},{9,13},{2,6},{6,10},{10,14},{3,7},{... | collective-permute-start | bytes 3145736 | tf_op jit(solution)/shard_map/ppermute | solution.py:82
  152.6 40.4 %collective-permute-start.18 = (bf16[1024,512]{1,0:T(8,128)(2,1)}, bf16[1024,512]{1,0:T(8,128)(2,1)S(1)}, u32[]{:S(2)}, u32[]{:S(2)}) collective-permute-start(bf16[1024,512]{1,0:T(8,128)(2,1)} %collective-permute-done.15), channel_id=1, source_target_pairs={{4,0},{8,4},{12,8},{5,1},{9,5},{13,9},{6,2},{10,6},{14,10},{7,3},{... | collective-permute-start | bytes 3145736 | tf_op jit(solution)/shard_map/ppermute | solution.py:83
  156.6 39.6 %collective-permute-start.5 = (bf16[1024,512]{1,0:T(8,128)(2,1)S(1)}, bf16[1024,512]{1,0:T(8,128)(2,1)S(1)}, u32[]{:S(2)}, u32[]{:S(2)}) collective-permute-start(bf16[1024,512]{1,0:T(8,128)(2,1)S(1)} %broadcast_select_fusion.1), channel_id=1, source_target_pairs={{0,16},{16,0},{1,17},{17,1},{2,18},{18,2},{3,19},{19,3},{4,20},{20... | collective-permute-start | bytes 3145736 | tf_op jit(solution)/shard_map/ppermute | solution.py:94
  167.6 37.7 %collective-permute-start.16 = (bf16[1024,512]{1,0:T(8,128)(2,1)S(1)}, bf16[1024,512]{1,0:T(8,128)(2,1)S(1)}, u32[]{:S(2)}, u32[]{:S(2)}) collective-permute-start(bf16[1024,512]{1,0:T(8,128)(2,1)S(1)} %broadcast_select_fusion), channel_id=1, source_target_pairs={{0,16},{16,0},{1,17},{17,1},{2,18},{18,2},{3,19},{19,3},{4,20},{20... | collective-permute-start | bytes 3145736 | tf_op jit(solution)/shard_map/ppermute | solution.py:94
  173.5 54.2 %collective-permute-start.2 = (bf16[1024,512]{1,0:T(8,128)(2,1)S(1)}, bf16[1024,512]{1,0:T(8,128)(2,1)S(1)}, u32[]{:S(2)}, u32[]{:S(2)}) collective-permute-start(bf16[1024,512]{1,0:T(8,128)(2,1)S(1)} %get-tuple-element.44), channel_id=1, source_target_pairs={{0,16},{16,0},{1,17},{17,1},{2,18},{18,2},{3,19},{19,3},{4,20},{20... | collective-permute-start | bytes 3145736 | tf_op jit(solution)/shard_map/ppermute | solution.py:94
  189.0 61.2 %collective-permute-start.8 = (bf16[1024,512]{1,0:T(8,128)(2,1)S(1)}, bf16[1024,512]{1,0:T(8,128)(2,1)S(1)}, u32[]{:S(2)}, u32[]{:S(2)}) collective-permute-start(bf16[1024,512]{1,0:T(8,128)(2,1)S(1)} %get-tuple-element.45), channel_id=1, source_target_pairs={{0,16},{16,0},{1,17},{17,1},{2,18},{18,2},{3,19},{19,3},{4,20},{20... | collective-permute-start | bytes 3145736 | tf_op jit(solution)/shard_map/ppermute | solution.py:94
  194.6 78.0 %collective-permute-start.13 = (bf16[1024,512]{1,0:T(8,128)(2,1)S(1)}, bf16[1024,512]{1,0:T(8,128)(2,1)S(1)}, u32[]{:S(2)}, u32[]{:S(2)}) collective-permute-start(bf16[1024,512]{1,0:T(8,128)(2,1)S(1)} %get-tuple-element.46), channel_id=1, source_target_pairs={{0,16},{16,0},{1,17},{17,1},{2,18},{18,2},{3,19},{19,3},{4,20},{20... | collective-permute-start | bytes 3145736 | tf_op jit(solution)/shard_map/ppermute | solution.py:94
  196.2 96.9 %collective-permute-start.19 = (bf16[1024,512]{1,0:T(8,128)(2,1)S(1)}, bf16[1024,512]{1,0:T(8,128)(2,1)S(1)}, u32[]{:S(2)}, u32[]{:S(2)}) collective-permute-start(bf16[1024,512]{1,0:T(8,128)(2,1)S(1)} %get-tuple-element.47), channel_id=1, source_target_pairs={{0,16},{16,0},{1,17},{17,1},{2,18},{18,2},{3,19},{19,3},{4,20},{20... | collective-permute-start | bytes 3145736 | tf_op jit(solution)/shard_map/ppermute | solution.py:94
  296.7 2.7 collective-permute-start.9
  297.8 6.3 %collective-permute-start.20 = (bf16[2,512,512]{1,2,0:T(8,128)(2,1)}, bf16[2,512,512]{1,2,0:T(8,128)(2,1)}, u32[]{:S(2)}, u32[]{:S(2)}) collective-permute-start(bf16[2,512,512]{1,2,0:T(8,128)(2,1)} %pad_maximum_fusion.4), channel_id=1, source_target_pairs={{0,1},{1,0},{2,3},{3,2},{4,5},{5,4},{6,7},{7,6},{8,9},{9,8},{10,11... | collective-permute-start | bytes 3145736 | tf_op jit(solution)/shard_map/ppermute | solution.py:124
  299.4 1.0 copy-start.6
  300.4 3.7 %copy-start.4 = (bf16[1,512,512]{1,2,0:T(8,128)(2,1)S(1)}, bf16[1,512,512]{1,2,0:T(8,128)(2,1)}, u32[]{:S(2)}) copy-start(bf16[1,512,512]{1,2,0:T(8,128)(2,1)} %get-tuple-element.43) | copy-start | bytes 1572868
  303.2 15.1 %collective-permute-start.10 = (bf16[512,512]{0,1:T(8,128)(2,1)}, bf16[512,512]{0,1:T(8,128)(2,1)}, u32[]{:S(2)}, u32[]{:S(2)}) collective-permute-start(bf16[512,512]{0,1:T(8,128)(2,1)} %fusion.43), channel_id=1, source_target_pairs={{0,2},{2,0},{1,3},{3,1},{4,6},{6,4},{5,7},{7,5},{8,10},{10,8},{9,1... | collective-permute-start | bytes 1572872 | tf_op jit(solution)/shard_map/ppermute | solution.py:128
  305.7 1.3 copy-start.1
  307.1 21.6 %collective-permute-start.21 = (bf16[512,512]{0,1:T(8,128)(2,1)S(1)}, bf16[512,512]{0,1:T(8,128)(2,1)}, u32[]{:S(2)}, u32[]{:S(2)}) collective-permute-start(bf16[512,512]{0,1:T(8,128)(2,1)S(1)} %fusion.44), channel_id=1, source_target_pairs={{0,2},{2,0},{1,3},{3,1},{4,6},{6,4},{5,7},{7,5},{8,10},{10,8},{9,1... | collective-permute-start | bytes 1572872 | tf_op jit(solution)/shard_map/ppermute | solution.py:128
  308.3 20.5 %copy-start.2 = (f32[2,512,512]{1,2,0:T(8,128)S(1)}, f32[2,512,512]{1,2,0:T(8,128)}, u32[]{:S(2)}) copy-start(f32[2,512,512]{1,2,0:T(8,128)} %copy-done.1) | copy-start | bytes 6291460
